TPU v7x, 256 devices: a whole 4x4x8 slice. The times are simulated.
256 devices in a mesh: pipe: 16 (over x, y_lo, core), tensor: 16 (over z, y_hi).
Axes of the slice: x: 4, y: 4 (y_hi: 2, y_lo: 2; y = y_hi * 2 + y_lo), z: 8, core: 2. Of those that a mesh axis runs over, the one named last changes fastest.
Arguments:
- q_fwd: bfloat16 [16, 256, 6144], P('pipe', None, 'tensor'), may hold values from -9 to 9
- k_fwd: bfloat16 [16, 256, 6144], P('pipe', None, 'tensor'), may hold values from -4 to 4
- v_fwd: bfloat16 [16, 256, 6144], P('pipe', None, 'tensor'), may hold values from -6 to 6
- q_park: bfloat16 [16, 256, 6144], P('pipe', None, 'tensor'), may hold values from -9 to 9
- k_park: bfloat16 [16, 256, 6144], P('pipe', None, 'tensor'), may hold values from -4 to 4
- v_park: bfloat16 [16, 256, 6144], P('pipe', None, 'tensor'), may hold values from -6 to 6
- resid: bfloat16 [16, 256, 12288], P('pipe', 'tensor'), may hold values from -6 to 6
- out_weight: bfloat16 [16, 6144, 12288], P('pipe', 'tensor'), may hold values from -0.078125 to 0.078125
- cotangent: bfloat16 [16, 256, 12288], P('pipe', 'tensor'), may hold values from -6 to 6
Outputs:
- output: bfloat16 [16, 256, 12288], P('pipe', 'tensor')
- grad_q: bfloat16 [16, 256, 6144], P('pipe', None, 'tensor')
- grad_k: bfloat16 [16, 256, 6144], P('pipe', None, 'tensor')
- grad_v: bfloat16 [16, 256, 6144], P('pipe', None, 'tensor')
- evict_q: bfloat16 [16, 256, 6144], P('pipe', None, 'tensor')
- evict_k: bfloat16 [16, 256, 6144], P('pipe', None, 'tensor')
- evict_v: bfloat16 [16, 256, 6144], P('pipe', None, 'tensor')
All inputs are finite; a program needn't handle non-finite values.
Results may differ from a plain program's by a relative error of at most 0.025.
Values may be sent and summed in bfloat16 or wider, within the bound.
A program may use at most 128 MiB of HBM per device.

v0:
```python
import jax
import jax.numpy as jnp
from jax import lax
from jax.sharding import PartitionSpec as P

HEAD = 128


def partner(x, axis, distance):
    return lax.ppermute(x, axis, [(i, i ^ 1 << distance) for i in range(lax.axis_size(axis))])


def probabilities(queries, keys_in):
    seq_length = queries.shape[0]
    head_width = queries.shape[-1]
    scores = jnp.einsum(
        "qhd,khd->hqk", queries, keys_in, preferred_element_type=jnp.float32
    ) * head_width ** (-0.5)
    causal = lax.broadcasted_iota(jnp.int32, (seq_length, seq_length), 0) >= lax.broadcasted_iota(
        jnp.int32, (seq_length, seq_length), 1
    )
    scores = jnp.where(causal[None], scores, jnp.float32(-1e30))
    biggest = jnp.max(scores, axis=-1, keepdims=True)
    exponent = jnp.exp(scores - biggest)
    attn_probs = exponent / jnp.sum(exponent, axis=-1, keepdims=True)
    return (attn_probs, attn_probs.astype(jnp.bfloat16))


def split_heads(block):
    return block.reshape(block.shape[0], -1, HEAD)


def per_device(q_fwd, k_fwd, v_fwd, q_park, k_park, v_park, resid, out_weight, cotangent):
    stacked = jnp.stack([q_fwd[0], k_fwd[0], v_fwd[0], q_park[0], k_park[0], v_park[0]])
    section_count = lax.axis_size("pipe")
    for bit_place in range(section_count.bit_length() - 1):
        stacked = partner(stacked, "pipe", bit_place)
    weight = out_weight[0]
    seq_length = q_fwd.shape[1]
    row_count = resid.shape[1]
    attn_probs, attn_low = probabilities(split_heads(q_fwd[0]), split_heads(k_fwd[0]))
    context = jnp.einsum(
        "hqk,khd->qhd", attn_low, split_heads(v_fwd[0]), preferred_element_type=jnp.float32
    )
    context = context.astype(jnp.bfloat16).reshape(seq_length, -1)
    full_sum = lax.psum(
        jnp.dot(context, weight, preferred_element_type=jnp.float32).astype(jnp.bfloat16), "tensor"
    ).astype(jnp.float32)
    own_rows = lax.dynamic_slice_in_dim(
        full_sum, lax.axis_index("tensor") * row_count, row_count, 0
    )
    output = (resid[0].astype(jnp.float32) + own_rows).astype(jnp.bfloat16)
    grad_ctx = lax.dot_general(
        lax.all_gather(cotangent[0], "tensor", axis=0, tiled=True),
        weight,
        (((1,), (1,)), ((), ())),
        preferred_element_type=jnp.float32,
    ).astype(jnp.bfloat16)
    q_heads = split_heads(stacked[3])
    k_heads = split_heads(stacked[4])
    v_heads = split_heads(stacked[5])
    grad_heads = split_heads(grad_ctx)
    back_probs, back_low = probabilities(q_heads, k_heads)
    recon = jnp.einsum(
        "hqk,khd->qhd", back_low, v_heads, preferred_element_type=jnp.float32
    ).astype(jnp.bfloat16)
    row_dots = jnp.sum(grad_heads.astype(jnp.float32) * recon.astype(jnp.float32), axis=-1)
    row_dots = jnp.transpose(row_dots)[:, :, None]
    grad_probs = jnp.einsum("qhd,khd->hqk", grad_heads, v_heads, preferred_element_type=jnp.float32)
    grad_scores = (back_probs * (grad_probs - row_dots)).astype(jnp.bfloat16)
    scale = HEAD ** (-0.5)
    grad_query = (
        jnp.einsum("hqk,khd->qhd", grad_scores, k_heads, preferred_element_type=jnp.float32) * scale
    ).astype(jnp.bfloat16)
    grad_key = (
        jnp.einsum("hqk,qhd->khd", grad_scores, q_heads, preferred_element_type=jnp.float32) * scale
    ).astype(jnp.bfloat16)
    grad_value = jnp.einsum(
        "hqk,qhd->khd", back_low, grad_heads, preferred_element_type=jnp.float32
    ).astype(jnp.bfloat16)
    return (
        output[None],
        grad_query.reshape(seq_length, -1)[None],
        grad_key.reshape(seq_length, -1)[None],
        grad_value.reshape(seq_length, -1)[None],
        stacked[0][None],
        stacked[1][None],
        stacked[2][None],
    )


def solution(mesh):
    placed = (
        P("pipe", None, "tensor"),
        P("pipe", None, "tensor"),
        P("pipe", None, "tensor"),
        P("pipe", None, "tensor"),
        P("pipe", None, "tensor"),
        P("pipe", None, "tensor"),
        P("pipe", "tensor", None),
        P("pipe", "tensor", None),
        P("pipe", "tensor", None),
    )
    return jax.shard_map(
        per_device,
        mesh=mesh,
        in_specs=placed,
        out_specs=(
            P("pipe", "tensor", None),
            P("pipe", None, "tensor"),
            P("pipe", None, "tensor"),
            P("pipe", None, "tensor"),
            P("pipe", None, "tensor"),
            P("pipe", None, "tensor"),
            P("pipe", None, "tensor"),
        ),
        check_vma=False,
    )
```

profile of v0, /device:TPU:1, one launch (start us, length us, event | category | flops | bytes accessed | tf_op | source)
XLA Modules:
  0.0 467.8 jit_solution(10082827185400719738)
XLA Ops:
  7.2 0.0 all-reduce.2.cloned.1.call-start
  7.2 1.1 copy.34
  8.3 1.1 copy.35
  9.4 0.0 copy-start.1
  9.4 0.5 fusion.37
  9.9 0.3 fusion.12
  10.2 0.1 copy-done.1
  10.3 0.1 copy.38
  10.5 0.3 convolution_convert_fusion.1
  10.8 9.1 %convolution_convert_fusion = bf16[256,12288]{1,0:T(8,128)(2,1)} fusion(bf16[256,384]{0,1:T(8,128)(2,1)S(1)} %bitcast.79, bf16[1,384,12288]{2,1,0:T(8,128)(2,1)} %param.16), kind=kOutput, calls=%fused_computation.2 | convolution fusion | flops 2419064832 | bytes 15925248 | tf_op jit(solution)/shard_map/dot_general | solution.py:47
  19.9 0.0 copy-start.2
  19.9 0.0 copy-start.3
  19.9 0.0 all-reduce.2.cloned.1.call-update
  19.9 0.0 copy-start.4
  19.9 0.0 all-gather.3.cloned.1.call-start
  20.0 0.7 all-gather.3.cloned.1.call-update
  20.7 0.1 copy-done.2
  20.8 0.1 copy.43
  20.9 0.0 copy-done.3
  21.0 0.1 copy.44
  21.1 0.0 copy-done.4
  21.1 0.1 copy.45
  21.4 3.3 collective-permute-start
  24.7 2.5 collective-permute-done
  27.2 0.0 collective-permute-start.1
  27.2 63.3 %collective-permute-done.1 = bf16[6,256,384]{1,2,0:T(8,128)(2,1)S(1)} collective-permute-done((bf16[6,256,384]{1,2,0:T(8,128)(2,1)S(1)}, bf16[6,256,384]{1,2,0:T(8,128)(2,1)S(1)}, u32[]{:S(2)}, u32[]{:S(2)}) %collective-permute-start.1) | collective-permute-done | bytes 1179680 | tf_op jit(solution)/shard_map/ppermute | solution.py:10
  90.5 0.0 collective-permute-start.2
  90.5 23.8 %collective-permute-done.2 = bf16[6,256,384]{1,2,0:T(8,128)(2,1)S(1)} collective-permute-done((bf16[6,256,384]{1,2,0:T(8,128)(2,1)S(1)}, bf16[6,256,384]{1,2,0:T(8,128)(2,1)S(1)}, u32[]{:S(2)}, u32[]{:S(2)}) %collective-permute-start.2) | collective-permute-done | bytes 1179680 | tf_op jit(solution)/shard_map/ppermute | solution.py:10
  114.3 0.0 collective-permute-start.3
  114.4 21.9 %collective-permute-done.3 = bf16[6,256,384]{1,2,0:T(8,128)(2,1)S(1)} collective-permute-done((bf16[6,256,384]{1,2,0:T(8,128)(2,1)S(1)}, bf16[6,256,384]{1,2,0:T(8,128)(2,1)S(1)}, u32[]{:S(2)}, u32[]{:S(2)}) %collective-permute-start.3) | collective-permute-done | bytes 1179680 | tf_op jit(solution)/shard_map/ppermute | solution.py:10
  136.3 0.1 fusion.36
  136.3 0.8 copy.59
  137.1 0.0 copy-start
  137.2 0.8 copy.60
  138.0 0.8 copy.61
  138.8 0.5 fusion.38
  139.2 187.6 %all-reduce.2.cloned.1.call-done = bf16[256,12288]{1,0:T(8,128)(2,1)} async-done(((bf16[256,12288]{1,0:T(8,128)(2,1)}), bf16[256,12288]{1,0:T(8,128)(2,1)}) %all-reduce.2.cloned.1.call-update) | async-done | bytes 6291472 | tf_op jit(solution)/shard_map/psum | solution.py:46
  326.9 0.0 copy-done
  326.9 1.8 fusion.26
  328.7 118.6 %all-gather.3.cloned.1.call-done = bf16[1,256,12288]{2,1,0:T(8,128)(2,1)} async-done(((bf16[1,16,12288]{2,1,0:T(8,128)(2,1)}), bf16[1,256,12288]{2,1,0:T(8,128)(2,1)}) %all-gather.3.cloned.1.call-update) | async-done | bytes 6291472 | tf_op jit(solution)/shard_map/all_gather | solution.py:54
  447.3 8.9 %fusion.19 = bf16[256,384]{1,0:T(8,128)(2,1)S(1)} fusion(bf16[1,384,12288]{2,1,0:T(8,128)(2,1)} %param.16, bf16[1,256,12288]{2,1,0:T(8,128)(2,1)} %all-gather.3.cloned.1.call-done), kind=kOutput, calls=%fused_computation.28 | convolution fusion | flops 2416017408 | bytes 15925248 | tf_op jit(solution)/shard_map/dot_general | solution.py:53
  456.2 0.1 copy.48
  456.3 0.6 fusion.24
  457.0 0.3 fusion.13
  457.3 0.2 fusion.17
  457.5 0.3 fusion.18
  457.8 0.6 convolution_convert_fusion.2
  458.5 0.8 copy.56
  459.3 0.8 copy.57
  460.1 0.8 copy.58
  (7 shorter events, 0.1 us)
Async XLA Ops:
  7.2 319.7 %all-reduce.2.cloned.1.call-start = ((), (), s32[]{:S(2)}) async-start(), calls=%async_computation | async-start | bytes 12582912 | tf_op jit(solution)/shard_map/psum | solution.py:46
  9.4 0.9 copy-start.1
  19.9 0.9 copy-start.2
  19.9 1.1 copy-start.3
  19.9 1.2 copy-start.4
  19.9 427.3 %all-gather.3.cloned.1.call-start = ((), (), s32[]{:S(2)}) async-start(), calls=%async_computation.1 | async-start | bytes 6684672 | tf_op jit(solution)/shard_map/all_gather | solution.py:54
  21.4 5.8 %collective-permute-start = (bf16[6,256,384]{1,2,0:T(8,128)(2,1)S(1)}, bf16[6,256,384]{1,2,0:T(8,128)(2,1)S(1)}, u32[]{:S(2)}, u32[]{:S(2)}) collective-permute-start(bf16[6,256,384]{1,2,0:T(8,128)(2,1)S(1)} %constant_dynamic-update-slice_fusion), channel_id=1, source_target_pairs={{0,16},{16,0},{32,48},{48,32},{64,80},{80,64},{96,112},{112,96},{1... | collective-permute-start | bytes 3538952 | tf_op jit(solution)/shard_map/ppermute | solution.py:10
  27.2 63.3 %collective-permute-start.1 = (bf16[6,256,384]{1,2,0:T(8,128)(2,1)S(1)}, bf16[6,256,384]{1,2,0:T(8,128)(2,1)S(1)}, u32[]{:S(2)}, u32[]{:S(2)}) collective-permute-start(bf16[6,256,384]{1,2,0:T(8,128)(2,1)S(1)} %collective-permute-done), channel_id=1, source_target_pairs={{0,32},{16,48},{32,0},{48,16},{64,96},{80,112},{96,64},{112,80},{1... | collective-permute-start | bytes 3538952 | tf_op jit(solution)/shard_map/ppermute | solution.py:10
  90.5 23.8 %collective-permute-start.2 = (bf16[6,256,384]{1,2,0:T(8,128)(2,1)S(1)}, bf16[6,256,384]{1,2,0:T(8,128)(2,1)S(1)}, u32[]{:S(2)}, u32[]{:S(2)}) collective-permute-start(bf16[6,256,384]{1,2,0:T(8,128)(2,1)S(1)} %collective-permute-done.1), channel_id=1, source_target_pairs={{0,64},{16,80},{32,96},{48,112},{64,0},{80,16},{96,32},{112,48},{1... | collective-permute-start | bytes 3538952 | tf_op jit(solution)/shard_map/ppermute | solution.py:10
  114.3 21.9 %collective-permute-start.3 = (bf16[6,256,384]{1,2,0:T(8,128)(2,1)S(1)}, bf16[6,256,384]{1,2,0:T(8,128)(2,1)S(1)}, u32[]{:S(2)}, u32[]{:S(2)}) collective-permute-start(bf16[6,256,384]{1,2,0:T(8,128)(2,1)S(1)} %collective-permute-done.2), channel_id=1, source_target_pairs={{0,128},{16,144},{32,160},{48,176},{64,192},{80,208},{96,224},{112... | collective-permute-start | bytes 3538952 | tf_op jit(solution)/shard_map/ppermute | solution.py:10
  137.1 189.7 %copy-start = (bf16[1,16,12288]{2,1,0:T(8,128)(2,1)S(1)}, bf16[1,16,12288]{2,1,0:T(8,128)(2,1)}, u32[]{:S(2)}) copy-start(bf16[1,16,12288]{2,1,0:T(8,128)(2,1)} %param.15) | copy-start | bytes 1179652
Sparse Core Ops, SparseCore 0:
  20.0 306.7 all-reduce.1
  329.4 117.7 all-gather.2
where the time goes:
time: 468 us
  waiting for transfers between devices  418 us (89%)
  matrix products  21.7 us (5%)
  between operations  14.2 us (3%)
  local copies, waits for them, and re-layouts  8.21 us (2%)
    psum x1, waiting for transfers between devices, per_device(): lax.psum(jnp.dot(context, weight, preferred_element_type=jnp.float32).ast...  188 us
    all_gather x1, waiting for transfers between devices, per_device(): lax.all_gather(cotangent[0], 'tensor', axis=0, tiled=True)  119 us
    ppermute x4, waiting for transfers between devices, partner(): lax.ppermute(x, axis, [(i, i ^ 1 << distance) for i in range(lax.axis_siz...  111 us
  transfers between devices with their start and end apart: 6, of which 6 were waited for; matrix products, arithmetic and copies ran while one was open for 1% of the time, Pallas kernels for 0%

commit v1 on v0

v1 whole, which is shorter than its diff:
```python
import jax
import jax.numpy as jnp
from jax import lax
from jax.experimental import pallas as pl
from jax.experimental.pallas import tpu as pltpu
from jax.sharding import PartitionSpec as P

HEAD = 128
MESH = pl.DeviceIdType.MESH
CUT = 5120
TILE = 512
ORDER = (7, 1, 6, 2, 5, 3, 0, 4)


def slot(off, side):
    return 2 * ORDER.index(off % 8) + side


def kernel(
    q_in, k_in, v_in, qp_in, kp_in, vp_in, resid_in, w_in, cot_in,
    out_ref, gq_ref, gk_ref, gv_ref, eq_ref, ek_ref, ev_ref,
    w, g, part, za, zb, ya, yb, qf, kf, vf, qs, ks, vs, resid, ctx, ctxp, probs, recon, gctx, gout, out,
    load_sem, store_sem, agz_s, agz_r, agy_s, agy_r, rsz_s, rsz_r, rsy_s, rsy_r, mir_s, mir_r,
):
    width = w.shape[1]
    rows = resid.shape[0]
    seq = qf.shape[0]
    heads = qf.shape[1] // HEAD
    wide_b = width - CUT
    p, t = lax.axis_index("pipe"), lax.axis_index("tensor")
    z, line = lax.div(t, 2), lax.rem(t, 2)
    up = (p, lax.rem(z + 1, 8) * 2 + line)
    down = (p, lax.rem(z + 7, 8) * 2 + line)
    across = (p, z * 2 + 1 - line)
    mirror = (lax.axis_size("pipe") - 1 - p, t)
    ways = (up, down)

    def row_of(off, side):
        block = lax.rem(z + off % 8, 8) * 2 + lax.rem(line + side, 2)
        return pl.multiple_of(block * rows, rows)

    loads = {}

    def load(name, src, dst):
        loads[name] = pltpu.make_async_copy(src, dst, load_sem.at[len(loads)])
        loads[name].start()

    load("cot", cot_in.at[0], g.at[slot(0, 0)])
    load("q", q_in.at[0], qf)
    load("k", k_in.at[0], kf)
    load("v", v_in.at[0], vf)
    quarter = w.shape[0] // 4
    for i in range(4):
        load(f"w{i}", w_in.at[0, pl.ds(i * quarter, quarter)], w.at[pl.ds(i * quarter, quarter)])
    load("resid", resid_in.at[0], resid)

    def remote(src, dst, send, recv, device):
        return pltpu.make_async_remote_copy(
            src_ref=src, dst_ref=dst, send_sem=send, recv_sem=recv, device_id=device, device_id_type=MESH
        )

    cols_a = pl.ds(0, CUT)
    cols_b = pl.ds(CUT, wide_b)
    half_a = (pl.ds(0, CUT // 2), pl.ds(CUT // 2, CUT // 2))
    half_b = (pl.ds(CUT, wide_b // 2), pl.ds(CUT + wide_b // 2, wide_b // 2))
    half_zb = (pl.ds(0, wide_b // 2), pl.ds(wide_b // 2, wide_b // 2))
    sides = (0, 0, 1)

    agz, rsz = {}, {}
    for way in range(2):
        sign = -1 if way == 0 else 1
        for hop in range(4):
            for stream in range(3):
                n = (way * 4 + hop) * 3 + stream
                side = sides[stream]
                if hop < 3:
                    cols = cols_a if stream == 0 else cols_b
                else:
                    cols = half_a[way] if stream == 0 else half_b[way]
                agz[way, hop, stream] = remote(
                    g.at[slot(sign * hop, side), :, cols],
                    g.at[slot(sign * (hop + 1), side), :, cols],
                    agz_s.at[n], agz_r.at[n], ways[way],
                )
                if hop > 0:
                    cols = cols_a if stream == 0 else cols_b
                    land = za.at[way, hop] if stream == 0 else zb.at[way, hop, side]
                else:
                    cols = half_a[way] if stream == 0 else half_b[way]
                    land = za.at[way, hop, :, half_a[way]] if stream == 0 else zb.at[way, hop, side, :, half_zb[way]]
                rsz[way, hop, stream] = remote(
                    part.at[slot(-sign * (4 - hop), side), :, cols], land, rsz_s.at[n], rsz_r.at[n], ways[way]
                )
    agy, rsy = {}, {}
    for i, off in enumerate((0, 7, 1, 6, 2, 5, 3)):
        agy[off] = remote(
            g.at[slot(off, 0), :, cols_a], g.at[slot(off, 1), :, cols_a], agy_s.at[i], agy_r.at[i], across
        )
    for way in range(2):
        agy[4, way] = remote(
            g.at[slot(4, 0), :, half_a[way]], g.at[slot(4, 1), :, half_a[way]],
            agy_s.at[7 + way], agy_r.at[7 + way], across,
        )
    agy["b"] = remote(g.at[slot(0, 0), :, cols_b], g.at[slot(0, 1), :, cols_b], agy_s.at[9], agy_r.at[9], across)
    for off in range(8):
        rsy[off] = remote(part.at[slot(off, 1), :, cols_a], ya.at[off], rsy_s.at[off], rsy_r.at[off], across)
    rsy["b"] = remote(part.at[slot(0, 1), :, cols_b], yb, rsy_s.at[8], rsy_r.at[8], across)
    mir = [
        remote(src, dst, mir_s.at[i], mir_r.at[i], mirror)
        for i, (src, dst) in enumerate((
            (qp_in.at[0], qs), (kp_in.at[0], ks), (vp_in.at[0], vs),
            (q_in.at[0], eq_ref.at[0]), (k_in.at[0], ek_ref.at[0]), (v_in.at[0], ev_ref.at[0]),
        ))
    ]

    scale = HEAD**-0.5

    def softmax(queries, keys):
        scores = lax.dot_general(queries, keys, (((1,), (1,)), ((), ())), preferred_element_type=jnp.float32) * scale
        seen = lax.broadcasted_iota(jnp.int32, (seq, seq), 0) >= lax.broadcasted_iota(jnp.int32, (seq, seq), 1)
        scores = jnp.where(seen, scores, jnp.float32(-1e30))
        grown = jnp.exp(scores - jnp.max(scores, axis=-1, keepdims=True))
        return grown / jnp.sum(grown, axis=-1, keepdims=True)

    def forward_attention():
        for h in range(heads):
            cols = pl.ds(h * HEAD, HEAD)
            low = softmax(qf[:, cols], kf[:, cols]).astype(jnp.bfloat16)
            ctx[:, cols] = jnp.dot(low, vf[:, cols], preferred_element_type=jnp.float32).astype(jnp.bfloat16)
        for off in range(8):
            for side in range(2):
                ctxp[pl.ds(slot(off, side) * rows, rows), :] = ctx[pl.ds(row_of(off, side), rows), :]

    def project(first, last):
        @pl.loop(first // TILE, last // TILE)
        def _(i):
            cols = pl.ds(pl.multiple_of(i * TILE, TILE), TILE)
            made = jnp.dot(ctxp[...], w[:, cols], preferred_element_type=jnp.float32).astype(jnp.bfloat16)
            part[:, :, cols] = made.reshape(part.shape[0], rows, TILE)

    def gather_grad(group):
        def body(i, total):
            cols = pl.ds(pl.multiple_of(i * 1024, 1024), 1024)
            block = g[pl.ds(group * 4, 4), :, cols].reshape(4 * rows, 1024)
            return total + lax.dot_general(
                block, w[:, cols], (((1,), (1,)), ((), ())), preferred_element_type=jnp.float32
            )

        total = lax.fori_loop(0, width // 1024, body, jnp.zeros((4 * rows, w.shape[0]), jnp.float32))
        total = total.astype(jnp.bfloat16)
        for i in range(4):
            off, side = ORDER[2 * group + i // 2], i % 2
            gctx[pl.ds(row_of(off, side), rows), :] = total[i * rows : (i + 1) * rows]

    def stash_probs():
        for h in range(heads):
            cols = pl.ds(h * HEAD, HEAD)
            attn = softmax(qs[:, cols], ks[:, cols])
            probs[h] = attn
            recon[:, cols] = jnp.dot(
                attn.astype(jnp.bfloat16), vs[:, cols], preferred_element_type=jnp.float32
            ).astype(jnp.bfloat16)

    def backward_attention():
        for h in range(heads):
            cols = pl.ds(h * HEAD, HEAD)
            grad, attn = gctx[:, cols], probs[h]
            dots = jnp.sum(
                grad.astype(jnp.float32) * recon[:, cols].astype(jnp.float32), axis=-1, keepdims=True
            )
            grad_probs = lax.dot_general(
                grad, vs[:, cols], (((1,), (1,)), ((), ())), preferred_element_type=jnp.float32
            )
            grad_scores = (attn * (grad_probs - dots)).astype(jnp.bfloat16)
            gout[0, :, cols] = (
                jnp.dot(grad_scores, ks[:, cols], preferred_element_type=jnp.float32) * scale
            ).astype(jnp.bfloat16)
            gout[1, :, cols] = (
                lax.dot_general(
                    grad_scores, qs[:, cols], (((0,), (0,)), ((), ())), preferred_element_type=jnp.float32
                )
                * scale
            ).astype(jnp.bfloat16)
            gout[2, :, cols] = lax.dot_general(
                attn.astype(jnp.bfloat16), grad, (((0,), (0,)), ((), ())), preferred_element_type=jnp.float32
            ).astype(jnp.bfloat16)

    def add(dst, terms, first, last):
        @pl.loop(0, (last - first) // TILE)
        def _(i):
            at = first + i * TILE
            total = part[dst, :, pl.ds(pl.multiple_of(at, TILE), TILE)].astype(jnp.float32)
            for ref, shift in terms:
                total += ref[:, pl.ds(pl.multiple_of(at - shift, TILE), TILE)].astype(jnp.float32)
            part[dst, :, pl.ds(pl.multiple_of(at, TILE), TILE)] = total.astype(jnp.bfloat16)

    def reduce_a(hop):
        if hop == 0:
            rsy[4].wait_recv()
            add(slot(4, 0), [(ya.at[4], 0)], 0, CUT)
        for way in range(2):
            sign = -1 if way == 0 else 1
            off = (-sign * (4 - hop)) % 8
            if hop > 0:
                rsy[off].wait_recv()
                rsz[way, hop - 1, 0].wait_recv()
                if hop == 1:
                    middle = CUT // 2
                    first, last = (0, middle) if way == 0 else (middle, CUT)
                    add(slot(off, 0), [(ya.at[off], 0), (za.at[way, 0], 0)], first, last)
                    first, last = (middle, CUT) if way == 0 else (0, middle)
                    add(slot(off, 0), [(ya.at[off], 0)], first, last)
                else:
                    add(slot(off, 0), [(ya.at[off], 0), (za.at[way, hop - 1], 0)], 0, CUT)
            rsz[way, hop, 0].start()

    def reduce_b(hop, stream):
        side = sides[stream]
        for way in range(2):
            sign = -1 if way == 0 else 1
            off = (-sign * (4 - hop)) % 8
            if hop > 0:
                rsz[way, hop - 1, stream].wait_recv()
                middle = CUT + wide_b // 2
                first, last = CUT, width
                if hop == 1:
                    first, last = (CUT, middle) if way == 0 else (middle, width)
                add(slot(off, side), [(zb.at[way, hop - 1, side], CUT)], first, last)
            rsz[way, hop, stream].start()

    def gather_on(hop, stream):
        for way in range(2):
            sign = -1 if way == 0 else 1
            agz[way, hop, stream].wait_recv()
            if hop < 3:
                agz[way, hop + 1, stream].start()
            if stream == 0:
                agy[sign * (hop + 1) % 8 if hop < 3 else (4, way)].start()

    barrier = pltpu.get_barrier_semaphore()
    for device in (up, down, across, mirror):
        pl.semaphore_signal(barrier, inc=1, device_id=device, device_id_type=MESH)
    pl.semaphore_wait(barrier, 4)

    loads["cot"].wait()
    for way in range(2):
        for stream in range(2):
            agz[way, 0, stream].start()
    agy["b"].start()
    agy[0].start()
    for i in range(3):
        mir[i].start()

    for name in ("q", "k", "v"):
        loads[name].wait()
    forward_attention()
    agy["b"].wait_recv()
    for way in range(2):
        agz[way, 0, 2].start()
    for i in range(4):
        loads[f"w{i}"].wait()
    project(0, CUT)
    for off in (4, 3, 5, 2, 6, 1, 7, 0):
        rsy[off].start()
    project(CUT, width)
    reduce_b(0, 1)
    reduce_b(0, 2)

    for hop in range(4):
        for stream in range(3):
            gather_on(hop, stream)
        reduce_a(hop)
        if hop < 3:
            reduce_b(hop + 1, 1)
            reduce_b(hop + 1, 2)
        if hop == 0:
            for i in range(3, 6):
                mir[i].start()
        if hop == 1:
            agy[7].wait_recv()
            agy[1].wait_recv()
            gather_grad(0)
        if hop == 2:
            for i in range(3):
                mir[i].wait_recv()
            stash_probs()
            agy[6].wait_recv()
            agy[2].wait_recv()
            gather_grad(1)

    for way in range(2):
        rsz[way, 3, 2].wait_recv()
    add(slot(0, 1), [(zb.at[0, 3, 1], CUT), (zb.at[1, 3, 1], CUT)], CUT, width)
    rsy["b"].start()
    agy[5].wait_recv()
    agy[3].wait_recv()
    gather_grad(2)
    agy[0].wait_recv()
    for way in range(2):
        agy[4, way].wait_recv()
    gather_grad(3)
    backward_attention()
    stores = [
        pltpu.make_async_copy(gout.at[i], ref.at[0], store_sem.at[i]) for i, ref in enumerate((gq_ref, gk_ref, gv_ref))
    ]
    for copy in stores:
        copy.start()

    loads["resid"].wait()
    rsy[0].wait_recv()
    for way in range(2):
        rsz[way, 3, 0].wait_recv()
        rsz[way, 3, 1].wait_recv()
    rsy["b"].wait_recv()

    def finish(first, last, refs, shift):
        @pl.loop(0, (last - first) // TILE)
        def _(i):
            cols = pl.ds(pl.multiple_of(first + i * TILE, TILE), TILE)
            total = part[slot(0, 0), :, cols].astype(jnp.float32)
            for ref in refs:
                total += ref[:, pl.ds(pl.multiple_of(first - shift + i * TILE, TILE), TILE)].astype(jnp.float32)
            out[:, cols] = (resid[:, cols].astype(jnp.float32) + total).astype(jnp.bfloat16)

    finish(0, CUT, (ya.at[0], za.at[0, 3], za.at[1, 3]), 0)
    finish(CUT, width, (yb, zb.at[0, 3, 0], zb.at[1, 3, 0]), CUT)
    last = pltpu.make_async_copy(out, out_ref.at[0], store_sem.at[3])
    last.start()

    for i in range(3, 6):
        mir[i].wait_recv()
    for copies in (agz, rsz, agy, rsy):
        for copy in copies.values():
            copy.wait_send()
    for copy in mir:
        copy.wait_send()
    for copy in stores:
        copy.wait()
    last.wait()


def per_device(q_fwd, k_fwd, v_fwd, q_park, k_park, v_park, resid, out_weight, cotangent):
    seq, features = q_fwd.shape[1:]
    rows, width = resid.shape[1:]
    slots = seq // rows
    heads = features // HEAD
    low = jnp.bfloat16
    block = jax.ShapeDtypeStruct(q_fwd.shape, low)
    anywhere = pl.BlockSpec(memory_space=pl.ANY)
    sems = pltpu.SemaphoreType.DMA
    return pl.pallas_call(
        kernel,
        name="relay",
        out_shape=(jax.ShapeDtypeStruct(resid.shape, low),) + (block,) * 6,
        in_specs=[anywhere] * 9,
        out_specs=(anywhere,) * 7,
        scratch_shapes=[
            pltpu.VMEM((features, width), low),
            pltpu.VMEM((slots, rows, width), low),
            pltpu.VMEM((slots, rows, width), low),
            pltpu.VMEM((2, 4, rows, CUT), low),
            pltpu.VMEM((2, 4, 2, rows, width - CUT), low),
            pltpu.VMEM((8, rows, CUT), low),
            pltpu.VMEM((rows, width - CUT), low),
            *[pltpu.VMEM((seq, features), low) for _ in range(6)],
            pltpu.VMEM((rows, width), low),
            pltpu.VMEM((seq, features), low),
            pltpu.VMEM((seq, features), low),
            pltpu.VMEM((heads, seq, seq), jnp.float32),
            pltpu.VMEM((seq, features), low),
            pltpu.VMEM((seq, features), low),
            pltpu.VMEM((3, seq, features), low),
            pltpu.VMEM((rows, width), low),
            sems((9,)), sems((4,)), sems((24,)), sems((24,)), sems((10,)), sems((10,)),
            sems((24,)), sems((24,)), sems((9,)), sems((9,)), sems((6,)), sems((6,)),
        ],
        compiler_params=pltpu.CompilerParams(
            collective_id=0, has_side_effects=True, vmem_limit_bytes=56 * 2**20
        ),
    )(q_fwd, k_fwd, v_fwd, q_park, k_park, v_park, resid, out_weight, cotangent)


def solution(mesh):
    placed = (P("pipe", None, "tensor"),) * 6 + (P("pipe", "tensor", None),) * 3
    return jax.shard_map(
        per_device,
        mesh=mesh,
        in_specs=placed,
        out_specs=(P("pipe", "tensor", None),) + (P("pipe", None, "tensor"),) * 6,
        check_vma=False,
    )
```

time: 468 us -> 142 us (0.30)
  waiting for transfers between devices: 418 us -> 0 us
  Pallas kernels: 0 us -> 129 us
  matrix products: 21.7 us -> 0 us
  between operations: 14.2 us -> 0.65 us
    psum x1 -> x0, waiting for transfers between devices: 188 us -> none  [per_device(): lax.psum(jnp.dot(context, weight, preferred_element_type=jnp.float32).ast...]
    pallas_call x0 -> x1, Pallas kernels: none -> 129 us  [per_device(): pl.pallas_call(kernel, name='relay', out_shape=(jax.ShapeDtypeStruct(resi...]
    all_gather x1 -> x0, waiting for transfers between devices: 119 us -> none  [per_device(): lax.all_gather(cotangent[0], 'tensor', axis=0, tiled=True)]
    ppermute x4 -> x0, waiting for transfers between devices: 111 us -> none  [partner(): lax.ppermute(x, axis, [(i, i ^ 1 << distance) for i in range(lax.axis_siz...]
    dot_general x9 -> x0, matrix products: 20.7 us -> none  [the longest x1 9.06 us: per_device(): jnp.dot(context, weight, preferred_element_type=jnp.float32)]
    unnamed x27 -> x7, local copies, waits for them, and re-layouts: 7.97 us -> 11.5 us
  transfers between devices with their start and end apart: 6 -> 0, of which waited for: 6 -> 0; matrix products, arithmetic and copies ran while one was open for 1% -> 0% of each run, Pallas kernels for 0% -> 0%
where the time goes in v1:
time: 142 us; the launch traced here: 141 us
  Pallas kernels  129 us (91%)
  local copies, waits for them, and re-layouts  11.5 us (8%)
    pallas_call x1, Pallas kernels, per_device(): pl.pallas_call(kernel, name='relay', out_shape=(jax.ShapeDtypeStruct(resi...  129 us
    unnamed x7, local copies, waits for them, and re-layouts  11.5 us

profile of v1, /device:TPU:1, one launch (start us, length us, event | category | flops | bytes accessed | tf_op | source)
XLA Modules:
  0.0 141.3 jit_solution(5954744383018582013)
XLA Ops:
  0.6 129.1 %relay.1 = (bf16[1,16,12288]{2,1,0:T(8,128)(2,1)}, bf16[1,256,384]{2,1,0:T(8,128)(2,1)}, bf16[1,256,384]{2,1,0:T(8,128)(2,1)}, bf16[1,256,384]{2,1,0:T(8,128)(2,...) custom-call(bf16[1,256,384]{2,1,0:T(8,128)(2,1)} %q_in.1, ...), custom_call_target="tpu_custom_call" | custom-call | tf_op jit(solution)/shard_map/relay/pallas_call | solution.py:351
  129.8 1.8 %copy.23 = bf16[1,16,12288]{2,1,0:T(8,128)(2,1)} copy(bf16[1,16,12288]{2,1,0:T(8,128)(2,1)} %get-tuple-element.14) | data formatting | bytes 786432
  131.5 1.6 %copy.24 = bf16[1,256,384]{2,1,0:T(8,128)(2,1)} copy(bf16[1,256,384]{2,1,0:T(8,128)(2,1)} %get-tuple-element.15) | data formatting | bytes 393216
  133.2 1.6 %copy.25 = bf16[1,256,384]{2,1,0:T(8,128)(2,1)} copy(bf16[1,256,384]{2,1,0:T(8,128)(2,1)} %get-tuple-element.16) | data formatting | bytes 393216
  134.8 1.6 %copy.26 = bf16[1,256,384]{2,1,0:T(8,128)(2,1)} copy(bf16[1,256,384]{2,1,0:T(8,128)(2,1)} %get-tuple-element.17) | data formatting | bytes 393216
  136.4 1.6 %copy.27 = bf16[1,256,384]{2,1,0:T(8,128)(2,1)} copy(bf16[1,256,384]{2,1,0:T(8,128)(2,1)} %get-tuple-element.18) | data formatting | bytes 393216
  138.0 1.6 %copy.28 = bf16[1,256,384]{2,1,0:T(8,128)(2,1)} copy(bf16[1,256,384]{2,1,0:T(8,128)(2,1)} %get-tuple-element.19) | data formatting | bytes 393216
  139.7 1.6 %copy.29 = bf16[1,256,384]{2,1,0:T(8,128)(2,1)} copy(bf16[1,256,384]{2,1,0:T(8,128)(2,1)} %get-tuple-element.20) | data formatting | bytes 393216

commit v2 on v1

--- a/solution.py
+++ b/solution.py
@@ -8,18 +8,34 @@
 HEAD = 128
 MESH = pl.DeviceIdType.MESH
 CUT = 5120
-TILE = 512
-ORDER = (7, 1, 6, 2, 5, 3, 0, 4)
+TILE = 1024
+STEP = 512
+PLAN = (
+    ("cross",), ("cross0",), ("send", 0, 1), ("send", 1, 1), ("forward",), ("send", 1, 0), ("send", 0, 0),
+    ("mirror", 2), ("gather", 0, 1, 0), ("gather", 0, 1, 1), ("project_b",), ("project_a",), ("reduce_b", 0, 1, 0),
+    ("mirror", 3), ("part", 4), ("crossed",), ("part", 2), ("part", 3), ("gather", 1, 1, 1), ("gather", 0, 0, 1),
+    ("reduce_b", 0, 2, 0), ("reduce_b", 1, 1, 0), ("mirror", 0), ("gather", 0, 0, 0), ("gather", 0, 2, 1),
+    ("gather", 2, 1, 1), ("gather", 1, 1, 0), ("reduce_b", 0, 2, 1), ("gather", 1, 0, 1), ("reduce_a0",),
+    ("reduce_b", 0, 1, 1), ("gather", 1, 0, 0), ("reduce_b", 1, 2, 1), ("gather", 0, 2, 0), ("reduce_a", 1, 0),
+    ("mirror", 5), ("part", 5), ("mirror", 1), ("gather", 1, 2, 1), ("gather", 2, 1, 0), ("part", 0), ("part", 6),
+    ("reduce_b", 1, 1, 1), ("gather", 2, 0, 1), ("reduce_b", 1, 2, 0), ("gather", 1, 2, 0), ("reduce_b", 2, 2, 1),
+    ("reduce_a", 1, 1), ("reduce_b", 2, 2, 0), ("reduce_b", 2, 1, 1), ("gather", 3, 1, 1), ("gather", 3, 0, 1),
+    ("gather", 2, 0, 0), ("gather", 2, 2, 1), ("gather", 2, 2, 0), ("part", 7), ("stash",), ("gather", 3, 1, 0),
+    ("reduce_b", 2, 1, 0), ("gather", 3, 0, 0), ("reduce_a", 2, 1), ("reduce_b", 3, 2, 0), ("reduce_b", 3, 2, 1),
+    ("mirror", 4), ("reduce_a", 2, 0), ("grad_a",), ("gather", 3, 2, 0), ("reduce_a", 3, 1), ("gather", 3, 2, 1),
+    ("part", 1), ("reduce_b", 3, 1, 0), ("sum_b",), ("reduce_b", 3, 1, 1), ("reduce_a", 3, 0), ("grad_b",),
+    ("backward",),
+)
 
 
 def slot(off, side):
-    return 2 * ORDER.index(off % 8) + side
+    return side * 8 + off % 8
 
 
 def kernel(
     q_in, k_in, v_in, qp_in, kp_in, vp_in, resid_in, w_in, cot_in,
     out_ref, gq_ref, gk_ref, gv_ref, eq_ref, ek_ref, ev_ref,
-    w, g, part, za, zb, ya, yb, qf, kf, vf, qs, ks, vs, resid, ctx, ctxp, probs, recon, gctx, gout, out,
+    w, g, part, za, zb, ya, yb, qf, kf, vf, qs, ks, vs, parked, evicted, resid, ctx, ctxp, probs, recon, total, gctx, gout, out,
     load_sem, store_sem, agz_s, agz_r, agy_s, agy_r, rsz_s, rsz_r, rsy_s, rsy_r, mir_s, mir_r,
 ):
     width = w.shape[1]
@@ -46,6 +62,8 @@
         loads[name].start()
 
     load("cot", cot_in.at[0], g.at[slot(0, 0)])
+    for i, ref in enumerate((qp_in, kp_in, vp_in)):
+        load(f"p{i}", ref.at[0], parked.at[i])
     load("q", q_in.at[0], qf)
     load("k", k_in.at[0], kf)
     load("v", v_in.at[0], vf)
@@ -108,8 +126,8 @@
     mir = [
         remote(src, dst, mir_s.at[i], mir_r.at[i], mirror)
         for i, (src, dst) in enumerate((
-            (qp_in.at[0], qs), (kp_in.at[0], ks), (vp_in.at[0], vs),
-            (q_in.at[0], eq_ref.at[0]), (k_in.at[0], ek_ref.at[0]), (v_in.at[0], ev_ref.at[0]),
+            (parked.at[0], qs), (parked.at[1], ks), (parked.at[2], vs),
+            (qf, evicted.at[0]), (kf, evicted.at[1]), (vf, evicted.at[2]),
         ))
     ]
 
@@ -138,19 +156,19 @@
             made = jnp.dot(ctxp[...], w[:, cols], preferred_element_type=jnp.float32).astype(jnp.bfloat16)
             part[:, :, cols] = made.reshape(part.shape[0], rows, TILE)
 
-    def gather_grad(group):
-        def body(i, total):
-            cols = pl.ds(pl.multiple_of(i * 1024, 1024), 1024)
-            block = g[pl.ds(group * 4, 4), :, cols].reshape(4 * rows, 1024)
-            return total + lax.dot_general(
-                block, w[:, cols], (((1,), (1,)), ((), ())), preferred_element_type=jnp.float32
+    def gather_grad(first, last):
+        @pl.loop(first // TILE, last // TILE)
+        def _(i):
+            cols = pl.ds(pl.multiple_of(i * TILE, TILE), TILE)
+            total[...] += lax.dot_general(
+                g[:, :, cols].reshape(seq, TILE), w[:, cols], (((1,), (1,)), ((), ())), preferred_element_type=jnp.float32
             )
 
-        total = lax.fori_loop(0, width // 1024, body, jnp.zeros((4 * rows, w.shape[0]), jnp.float32))
-        total = total.astype(jnp.bfloat16)
-        for i in range(4):
-            off, side = ORDER[2 * group + i // 2], i % 2
-            gctx[pl.ds(row_of(off, side), rows), :] = total[i * rows : (i + 1) * rows]
+    def spread_grad():
+        for off in range(8):
+            for side in range(2):
+                rows_here = pl.ds(slot(off, side) * rows, rows)
+                gctx[pl.ds(row_of(off, side), rows), :] = total[rows_here, :].astype(jnp.bfloat16)
 
     def stash_probs():
         for h in range(heads):
@@ -186,56 +204,104 @@
             ).astype(jnp.bfloat16)
 
     def add(dst, terms, first, last):
-        @pl.loop(0, (last - first) // TILE)
+        @pl.loop(0, (last - first) // STEP)
         def _(i):
-            at = first + i * TILE
-            total = part[dst, :, pl.ds(pl.multiple_of(at, TILE), TILE)].astype(jnp.float32)
+            at = first + i * STEP
+            total = part[dst, :, pl.ds(pl.multiple_of(at, STEP), STEP)].astype(jnp.float32)
             for ref, shift in terms:
-                total += ref[:, pl.ds(pl.multiple_of(at - shift, TILE), TILE)].astype(jnp.float32)
-            part[dst, :, pl.ds(pl.multiple_of(at, TILE), TILE)] = total.astype(jnp.bfloat16)
-
-    def reduce_a(hop):
-        if hop == 0:
+                total += ref[:, pl.ds(pl.multiple_of(at - shift, STEP), STEP)].astype(jnp.float32)
+            part[dst, :, pl.ds(pl.multiple_of(at, STEP), STEP)] = total.astype(jnp.bfloat16)
+
+    def reduce_a(hop, way):
+        off = (4 - hop) * (1 if way == 0 else -1) % 8
+        here, middle = slot(off, 0), CUT // 2
+        left, right = (0, middle), (middle, CUT)
+        rsy[off].wait_recv()
+        rsz[way, hop - 1, 0].wait_recv()
+        if hop == 1:
+            add(here, [(ya.at[off], 0), (za.at[way, 0], 0)], *(left, right)[way])
+            add(here, [(ya.at[off], 0)], *(right, left)[way])
+        else:
+            add(here, [(ya.at[off], 0), (za.at[way, hop - 1], 0)], 0, CUT)
+        rsz[way, hop, 0].start()
+
+    def reduce_b(hop, stream, way):
+        side = sides[stream]
+        off = (4 - hop) * (1 if way == 0 else -1) % 8
+        if hop > 0:
+            rsz[way, hop - 1, stream].wait_recv()
+            middle = CUT + wide_b // 2
+            first, last = ((CUT, middle), (middle, width))[way] if hop == 1 else (CUT, width)
+            add(slot(off, side), [(zb.at[way, hop - 1, side], CUT)], first, last)
+        rsz[way, hop, stream].start()
+
+    def gather_on(hop, stream, way):
+        agz[way, hop, stream].wait_recv()
+        if hop < 3:
+            agz[way, hop + 1, stream].start()
+        if stream == 0:
+            agy[(-1 if way == 0 else 1) * (hop + 1) % 8 if hop < 3 else (4, way)].start()
+
+    def act(what, *at):
+        if what == "send":
+            agz[at[0], 0, at[1]].start()
+        elif what == "cross":
+            agy["b"].start()
+        elif what == "cross0":
+            agy[0].start()
+        elif what == "mirror":
+            if at[0] < 3:
+                loads[f"p{at[0]}"].wait()
+            mir[at[0]].start()
+        elif what == "forward":
+            for name in ("q", "k", "v"):
+                loads[name].wait()
+            forward_attention()
+        elif what == "crossed":
+            agy["b"].wait_recv()
+            for way in range(2):
+                agz[way, 0, 2].start()
+        elif what in ("project_b", "project_a"):
+            if what == next(step[0] for step in PLAN if step[0].startswith("project")):
+                for i in range(4):
+                    loads[f"w{i}"].wait()
+            project(*((0, CUT) if what == "project_a" else (CUT, width)))
+        elif what == "part":
+            rsy[at[0]].start()
+        elif what == "gather":
+            gather_on(*at)
+        elif what == "reduce_b":
+            reduce_b(*at)
+        elif what == "reduce_a0":
             rsy[4].wait_recv()
             add(slot(4, 0), [(ya.at[4], 0)], 0, CUT)
-        for way in range(2):
-            sign = -1 if way == 0 else 1
-            off = (-sign * (4 - hop)) % 8
-            if hop > 0:
-                rsy[off].wait_recv()
-                rsz[way, hop - 1, 0].wait_recv()
-                if hop == 1:
-                    middle = CUT // 2
-                    first, last = (0, middle) if way == 0 else (middle, CUT)
-                    add(slot(off, 0), [(ya.at[off], 0), (za.at[way, 0], 0)], first, last)
-                    first, last = (middle, CUT) if way == 0 else (0, middle)
-                    add(slot(off, 0), [(ya.at[off], 0)], first, last)
-                else:
-                    add(slot(off, 0), [(ya.at[off], 0), (za.at[way, hop - 1], 0)], 0, CUT)
-            rsz[way, hop, 0].start()
-
-    def reduce_b(hop, stream):
-        side = sides[stream]
-        for way in range(2):
-            sign = -1 if way == 0 else 1
-            off = (-sign * (4 - hop)) % 8
-            if hop > 0:
-                rsz[way, hop - 1, stream].wait_recv()
-                middle = CUT + wide_b // 2
-                first, last = CUT, width
-                if hop == 1:
-                    first, last = (CUT, middle) if way == 0 else (middle, width)
-                add(slot(off, side), [(zb.at[way, hop - 1, side], CUT)], first, last)
-            rsz[way, hop, stream].start()
-
-    def gather_on(hop, stream):
-        for way in range(2):
-            sign = -1 if way == 0 else 1
-            agz[way, hop, stream].wait_recv()
-            if hop < 3:
-                agz[way, hop + 1, stream].start()
-            if stream == 0:
-                agy[sign * (hop + 1) % 8 if hop < 3 else (4, way)].start()
+            for way in range(2):
+                rsz[way, 0, 0].start()
+        elif what == "reduce_a":
+            reduce_a(*at)
+        elif what == "sum_b":
+            for way in range(2):
+                rsz[way, 3, 2].wait_recv()
+            add(slot(0, 1), [(zb.at[0, 3, 1], CUT), (zb.at[1, 3, 1], CUT)], CUT, width)
+            rsy["b"].start()
+        elif what == "stash":
+            for i in range(3):
+                mir[i].wait_recv()
+            stash_probs()
+        elif what == "grad_b":
+            gather_grad(CUT, width)
+        elif what == "grad_a":
+            for off in (0, 7, 1, 6, 2, 5, 3):
+                agy[off].wait_recv()
+            for way in range(2):
+                agy[4, way].wait_recv()
+            gather_grad(0, CUT)
+        elif what == "backward":
+            spread_grad()
+            backward_attention()
+            for i, ref in enumerate((gq_ref, gk_ref, gv_ref)):
+                stores.append(pltpu.make_async_copy(gout.at[i], ref.at[0], store_sem.at[i]))
+                stores[-1].start()
 
     barrier = pltpu.get_barrier_semaphore()
     for device in (up, down, across, mirror):
@@ -243,68 +309,10 @@
     pl.semaphore_wait(barrier, 4)
 
     loads["cot"].wait()
-    for way in range(2):
-        for stream in range(2):
-            agz[way, 0, stream].start()
-    agy["b"].start()
-    agy[0].start()
-    for i in range(3):
-        mir[i].start()
-
-    for name in ("q", "k", "v"):
-        loads[name].wait()
-    forward_attention()
-    agy["b"].wait_recv()
-    for way in range(2):
-        agz[way, 0, 2].start()
-    for i in range(4):
-        loads[f"w{i}"].wait()
-    project(0, CUT)
-    for off in (4, 3, 5, 2, 6, 1, 7, 0):
-        rsy[off].start()
-    project(CUT, width)
-    reduce_b(0, 1)
-    reduce_b(0, 2)
-
-    for hop in range(4):
-        for stream in range(3):
-            gather_on(hop, stream)
-        reduce_a(hop)
-        if hop < 3:
-            reduce_b(hop + 1, 1)
-            reduce_b(hop + 1, 2)
-        if hop == 0:
-            for i in range(3, 6):
-                mir[i].start()
-        if hop == 1:
-            agy[7].wait_recv()
-            agy[1].wait_recv()
-            gather_grad(0)
-        if hop == 2:
-            for i in range(3):
-                mir[i].wait_recv()
-            stash_probs()
-            agy[6].wait_recv()
-            agy[2].wait_recv()
-            gather_grad(1)
-
-    for way in range(2):
-        rsz[way, 3, 2].wait_recv()
-    add(slot(0, 1), [(zb.at[0, 3, 1], CUT), (zb.at[1, 3, 1], CUT)], CUT, width)
-    rsy["b"].start()
-    agy[5].wait_recv()
-    agy[3].wait_recv()
-    gather_grad(2)
-    agy[0].wait_recv()
-    for way in range(2):
-        agy[4, way].wait_recv()
-    gather_grad(3)
-    backward_attention()
-    stores = [
-        pltpu.make_async_copy(gout.at[i], ref.at[0], store_sem.at[i]) for i, ref in enumerate((gq_ref, gk_ref, gv_ref))
-    ]
-    for copy in stores:
-        copy.start()
+    total[...] = jnp.zeros_like(total)
+    stores = []
+    for step in PLAN:
+        act(*step)
 
     loads["resid"].wait()
     rsy[0].wait_recv()
@@ -314,12 +322,12 @@
     rsy["b"].wait_recv()
 
     def finish(first, last, refs, shift):
-        @pl.loop(0, (last - first) // TILE)
+        @pl.loop(0, (last - first) // STEP)
         def _(i):
-            cols = pl.ds(pl.multiple_of(first + i * TILE, TILE), TILE)
+            cols = pl.ds(pl.multiple_of(first + i * STEP, STEP), STEP)
             total = part[slot(0, 0), :, cols].astype(jnp.float32)
             for ref in refs:
-                total += ref[:, pl.ds(pl.multiple_of(first - shift + i * TILE, TILE), TILE)].astype(jnp.float32)
+                total += ref[:, pl.ds(pl.multiple_of(first - shift + i * STEP, STEP), STEP)].astype(jnp.float32)
             out[:, cols] = (resid[:, cols].astype(jnp.float32) + total).astype(jnp.bfloat16)
 
     finish(0, CUT, (ya.at[0], za.at[0, 3], za.at[1, 3]), 0)
@@ -327,8 +335,10 @@
     last = pltpu.make_async_copy(out, out_ref.at[0], store_sem.at[3])
     last.start()
 
-    for i in range(3, 6):
-        mir[i].wait_recv()
+    for i, ref in enumerate((eq_ref, ek_ref, ev_ref)):
+        mir[3 + i].wait_recv()
+        stores.append(pltpu.make_async_copy(evicted.at[i], ref.at[0], store_sem.at[4 + i]))
+        stores[-1].start()
     for copies in (agz, rsz, agy, rsy):
         for copy in copies.values():
             copy.wait_send()
@@ -337,6 +347,20 @@
     for copy in stores:
         copy.wait()
     last.wait()
+
+
+def place(*refs):
+    count = len(refs) // 3
+    sem_in, sem_out = refs[-2:]
+    comes = [pltpu.make_async_copy(refs[i], refs[2 * count + i], sem_in.at[i]) for i in range(count)]
+    goes = [pltpu.make_async_copy(refs[2 * count + i], refs[count + i], sem_out.at[i]) for i in range(count)]
+    for copy in comes:
+        copy.start()
+    for i in range(count):
+        comes[i].wait()
+        goes[i].start()
+    for copy in goes:
+        copy.wait()
 
 
 def per_device(q_fwd, k_fwd, v_fwd, q_park, k_park, v_park, resid, out_weight, cotangent):
@@ -348,7 +372,7 @@
     block = jax.ShapeDtypeStruct(q_fwd.shape, low)
     anywhere = pl.BlockSpec(memory_space=pl.ANY)
     sems = pltpu.SemaphoreType.DMA
-    return pl.pallas_call(
+    made = pl.pallas_call(
         kernel,
         name="relay",
         out_shape=(jax.ShapeDtypeStruct(resid.shape, low),) + (block,) * 6,
@@ -363,21 +387,32 @@
             pltpu.VMEM((8, rows, CUT), low),
             pltpu.VMEM((rows, width - CUT), low),
             *[pltpu.VMEM((seq, features), low) for _ in range(6)],
+            pltpu.VMEM((3, seq, features), low),
+            pltpu.VMEM((3, seq, features), low),
             pltpu.VMEM((rows, width), low),
             pltpu.VMEM((seq, features), low),
             pltpu.VMEM((seq, features), low),
             pltpu.VMEM((heads, seq, seq), jnp.float32),
             pltpu.VMEM((seq, features), low),
+            pltpu.VMEM((seq, features), jnp.float32),
             pltpu.VMEM((seq, features), low),
             pltpu.VMEM((3, seq, features), low),
             pltpu.VMEM((rows, width), low),
-            sems((9,)), sems((4,)), sems((24,)), sems((24,)), sems((10,)), sems((10,)),
+            sems((12,)), sems((7,)), sems((24,)), sems((24,)), sems((10,)), sems((10,)),
             sems((24,)), sems((24,)), sems((9,)), sems((9,)), sems((6,)), sems((6,)),
         ],
         compiler_params=pltpu.CompilerParams(
             collective_id=0, has_side_effects=True, vmem_limit_bytes=56 * 2**20
         ),
     )(q_fwd, k_fwd, v_fwd, q_park, k_park, v_park, resid, out_weight, cotangent)
+    return pl.pallas_call(
+        place,
+        name="place",
+        out_shape=tuple(jax.ShapeDtypeStruct(x.shape, x.dtype) for x in made),
+        in_specs=[anywhere] * 7,
+        out_specs=(anywhere,) * 7,
+        scratch_shapes=[pltpu.VMEM(x.shape, x.dtype) for x in made] + [sems((7,)), sems((7,))],
+    )(*made)
 
 
 def solution(mesh):

time: 142 us -> 114 us (0.80)
  Pallas kernels: 129 us -> 113 us
  local copies, waits for them, and re-layouts: 11.5 us -> 0 us
    pallas_call x1, Pallas kernels: 129 us -> 111 us  [per_device(): pl.pallas_call(kernel, name='relay', out_shape=(jax.ShapeDtypeStruct(resi...]
    unnamed x7 -> x0, local copies, waits for them, and re-layouts: 11.5 us -> none
    pallas_call x0 -> x1, Pallas kernels: none -> 2.25 us  [per_device(): pl.pallas_call(place, name='place', out_shape=tuple((jax.ShapeDtypeStruct...]
where the time goes in v2:
time: 114 us
  Pallas kernels  113 us (99%)
    pallas_call x1, Pallas kernels, per_device(): pl.pallas_call(kernel, name='relay', out_shape=(jax.ShapeDtypeStruct(resi...  111 us

profile of v2, /device:TPU:1, one launch (start us, length us, event | category | flops | bytes accessed | tf_op | source)
XLA Modules:
  0.0 114.0 jit_solution(15871957644594293807)
XLA Ops:
  0.6 111.1 %relay.1 = (bf16[1,16,12288]{2,1,0:T(8,128)(2,1)}, bf16[1,256,384]{2,1,0:T(8,128)(2,1)}, bf16[1,256,384]{2,1,0:T(8,128)(2,1)}, bf16[1,256,384]{2,1,0:T(8,128)(2,...) custom-call(bf16[1,256,384]{2,1,0:T(8,128)(2,1)} %q_in.1, ...), custom_call_target="tpu_custom_call" | custom-call | tf_op jit(solution)/shard_map/relay/pallas_call | solution.py:375
  111.8 2.2 %place.1 = (bf16[1,16,12288]{2,1,0:T(8,128)(2,1)}, bf16[1,256,384]{2,1,0:T(8,128)(2,1)}, bf16[1,256,384]{2,1,0:T(8,128)(2,1)}, bf16[1,256,384]{2,1,0:T(8,128)(2,...) custom-call(bf16[1,16,12288]{2,1,0:T(8,128)(2,1)} %get-tuple-element.14.refs_0_, ...), custom_call_target="tpu_custom_call" | custom-call | tf_op jit(solution)/shard_map/place/pallas_call | solution.py:408

commit v3 on v2

--- a/solution.py
+++ b/solution.py
@@ -11,20 +11,19 @@
 TILE = 1024
 STEP = 512
 PLAN = (
-    ("cross",), ("cross0",), ("send", 0, 1), ("send", 1, 1), ("forward",), ("send", 1, 0), ("send", 0, 0),
-    ("mirror", 2), ("gather", 0, 1, 0), ("gather", 0, 1, 1), ("project_b",), ("project_a",), ("reduce_b", 0, 1, 0),
-    ("mirror", 3), ("part", 4), ("crossed",), ("part", 2), ("part", 3), ("gather", 1, 1, 1), ("gather", 0, 0, 1),
-    ("reduce_b", 0, 2, 0), ("reduce_b", 1, 1, 0), ("mirror", 0), ("gather", 0, 0, 0), ("gather", 0, 2, 1),
-    ("gather", 2, 1, 1), ("gather", 1, 1, 0), ("reduce_b", 0, 2, 1), ("gather", 1, 0, 1), ("reduce_a0",),
-    ("reduce_b", 0, 1, 1), ("gather", 1, 0, 0), ("reduce_b", 1, 2, 1), ("gather", 0, 2, 0), ("reduce_a", 1, 0),
-    ("mirror", 5), ("part", 5), ("mirror", 1), ("gather", 1, 2, 1), ("gather", 2, 1, 0), ("part", 0), ("part", 6),
-    ("reduce_b", 1, 1, 1), ("gather", 2, 0, 1), ("reduce_b", 1, 2, 0), ("gather", 1, 2, 0), ("reduce_b", 2, 2, 1),
-    ("reduce_a", 1, 1), ("reduce_b", 2, 2, 0), ("reduce_b", 2, 1, 1), ("gather", 3, 1, 1), ("gather", 3, 0, 1),
-    ("gather", 2, 0, 0), ("gather", 2, 2, 1), ("gather", 2, 2, 0), ("part", 7), ("stash",), ("gather", 3, 1, 0),
-    ("reduce_b", 2, 1, 0), ("gather", 3, 0, 0), ("reduce_a", 2, 1), ("reduce_b", 3, 2, 0), ("reduce_b", 3, 2, 1),
-    ("mirror", 4), ("reduce_a", 2, 0), ("grad_a",), ("gather", 3, 2, 0), ("reduce_a", 3, 1), ("gather", 3, 2, 1),
-    ("part", 1), ("reduce_b", 3, 1, 0), ("sum_b",), ("reduce_b", 3, 1, 1), ("reduce_a", 3, 0), ("grad_b",),
-    ("backward",),
+    ("mirror", 0), ("cross",), ("send", 0, 1), ("send", 1, 0), ("send", 0, 0), ("send", 1, 1), ("forward",),
+    ("project_b",), ("reduce_b", 0, 1, 1), ("mirror", 1), ("reduce_b", 0, 2, 0), ("project_a",), ("part", 3),
+    ("reduce_b", 0, 1, 0), ("gather", 0, 0, 1), ("reduce_b", 0, 2, 1), ("gather", 0, 1, 1), ("gather", 0, 0, 0),
+    ("crossed",), ("part", 4), ("part", 5), ("reduce_b", 1, 1, 1), ("reduce_b", 1, 2, 0), ("gather", 1, 0, 0),
+    ("part", 6), ("part", 7), ("gather", 0, 1, 0), ("mirror", 2), ("reduce_b", 1, 2, 1), ("reduce_b", 1, 1, 0),
+    ("gather", 1, 0, 1), ("reduce_a0",), ("gather", 0, 2, 0), ("part", 2), ("gather", 0, 2, 1), ("reduce_b", 2, 1, 1),
+    ("gather", 2, 0, 0), ("part", 0), ("reduce_b", 2, 2, 0), ("reduce_b", 2, 2, 1), ("reduce_a", 1, 0),
+    ("reduce_a", 1, 1), ("gather", 2, 0, 1), ("gather", 1, 1, 0), ("gather", 1, 2, 1), ("gather", 1, 2, 0),
+    ("mirror", 3), ("reduce_a", 2, 0), ("gather", 1, 1, 1), ("reduce_b", 2, 1, 0), ("reduce_b", 3, 2, 0), ("part", 1),
+    ("reduce_b", 3, 2, 1), ("cross0",), ("mirror", 4), ("reduce_a", 2, 1), ("gather", 3, 0, 1), ("gather", 2, 2, 1),
+    ("gather", 2, 2, 0), ("gather", 2, 1, 0), ("gather", 3, 0, 0), ("gather", 2, 1, 1), ("stash",), ("mirror", 5),
+    ("reduce_b", 3, 1, 0), ("reduce_a", 3, 0), ("reduce_b", 3, 1, 1), ("sum_b",), ("reduce_a", 3, 1), ("grad_a",),
+    ("gather", 3, 1, 0), ("gather", 3, 2, 0), ("gather", 3, 1, 1), ("gather", 3, 2, 1), ("grad_b",), ("backward",),
 )
 
 
@@ -35,8 +34,8 @@
 def kernel(
     q_in, k_in, v_in, qp_in, kp_in, vp_in, resid_in, w_in, cot_in,
     out_ref, gq_ref, gk_ref, gv_ref, eq_ref, ek_ref, ev_ref,
-    w, g, part, za, zb, ya, yb, qf, kf, vf, qs, ks, vs, parked, evicted, resid, ctx, ctxp, probs, recon, total, gctx, gout, out,
-    load_sem, store_sem, agz_s, agz_r, agy_s, agy_r, rsz_s, rsz_r, rsy_s, rsy_r, mir_s, mir_r,
+    w, g, part, za, zb, ya, yb, qf, kf, vf, qs, ks, vs, parked, resid, ctx, ctxp, probs, recon, total, gctx,
+    load_sem, agz_s, agz_r, agy_s, agy_r, rsz_s, rsz_r, rsy_s, rsy_r, mir_s, mir_r,
 ):
     width = w.shape[1]
     rows = resid.shape[0]
@@ -127,7 +126,7 @@
         remote(src, dst, mir_s.at[i], mir_r.at[i], mirror)
         for i, (src, dst) in enumerate((
             (parked.at[0], qs), (parked.at[1], ks), (parked.at[2], vs),
-            (qf, evicted.at[0]), (kf, evicted.at[1]), (vf, evicted.at[2]),
+            (qf, eq_ref.at[0]), (kf, ek_ref.at[0]), (vf, ev_ref.at[0]),
         ))
     ]
 
@@ -190,16 +189,16 @@
                 grad, vs[:, cols], (((1,), (1,)), ((), ())), preferred_element_type=jnp.float32
             )
             grad_scores = (attn * (grad_probs - dots)).astype(jnp.bfloat16)
-            gout[0, :, cols] = (
+            gq_ref[0, :, cols] = (
                 jnp.dot(grad_scores, ks[:, cols], preferred_element_type=jnp.float32) * scale
             ).astype(jnp.bfloat16)
-            gout[1, :, cols] = (
+            gk_ref[0, :, cols] = (
                 lax.dot_general(
                     grad_scores, qs[:, cols], (((0,), (0,)), ((), ())), preferred_element_type=jnp.float32
                 )
                 * scale
             ).astype(jnp.bfloat16)
-            gout[2, :, cols] = lax.dot_general(
+            gv_ref[0, :, cols] = lax.dot_general(
                 attn.astype(jnp.bfloat16), grad, (((0,), (0,)), ((), ())), preferred_element_type=jnp.float32
             ).astype(jnp.bfloat16)
 
@@ -299,9 +298,6 @@
         elif what == "backward":
             spread_grad()
             backward_attention()
-            for i, ref in enumerate((gq_ref, gk_ref, gv_ref)):
-                stores.append(pltpu.make_async_copy(gout.at[i], ref.at[0], store_sem.at[i]))
-                stores[-1].start()
 
     barrier = pltpu.get_barrier_semaphore()
     for device in (up, down, across, mirror):
@@ -310,7 +306,6 @@
 
     loads["cot"].wait()
     total[...] = jnp.zeros_like(total)
-    stores = []
     for step in PLAN:
         act(*step)
 
@@ -328,38 +323,26 @@
             total = part[slot(0, 0), :, cols].astype(jnp.float32)
             for ref in refs:
                 total += ref[:, pl.ds(pl.multiple_of(first - shift + i * STEP, STEP), STEP)].astype(jnp.float32)
-            out[:, cols] = (resid[:, cols].astype(jnp.float32) + total).astype(jnp.bfloat16)
+            out_ref[0, :, cols] = (resid[:, cols].astype(jnp.float32) + total).astype(jnp.bfloat16)
 
     finish(0, CUT, (ya.at[0], za.at[0, 3], za.at[1, 3]), 0)
     finish(CUT, width, (yb, zb.at[0, 3, 0], zb.at[1, 3, 0]), CUT)
-    last = pltpu.make_async_copy(out, out_ref.at[0], store_sem.at[3])
-    last.start()
-
-    for i, ref in enumerate((eq_ref, ek_ref, ev_ref)):
-        mir[3 + i].wait_recv()
-        stores.append(pltpu.make_async_copy(evicted.at[i], ref.at[0], store_sem.at[4 + i]))
-        stores[-1].start()
+
+    for i in range(3, 6):
+        mir[i].wait_recv()
     for copies in (agz, rsz, agy, rsy):
         for copy in copies.values():
             copy.wait_send()
     for copy in mir:
         copy.wait_send()
-    for copy in stores:
-        copy.wait()
-    last.wait()
 
 
 def place(*refs):
-    count = len(refs) // 3
-    sem_in, sem_out = refs[-2:]
-    comes = [pltpu.make_async_copy(refs[i], refs[2 * count + i], sem_in.at[i]) for i in range(count)]
-    goes = [pltpu.make_async_copy(refs[2 * count + i], refs[count + i], sem_out.at[i]) for i in range(count)]
-    for copy in comes:
+    count = len(refs) // 2
+    copies = [pltpu.make_async_copy(refs[i], refs[count + i], refs[-1].at[i]) for i in range(count)]
+    for copy in copies:
         copy.start()
-    for i in range(count):
-        comes[i].wait()
-        goes[i].start()
-    for copy in goes:
+    for copy in copies:
         copy.wait()
 
 
@@ -369,15 +352,14 @@
     slots = seq // rows
     heads = features // HEAD
     low = jnp.bfloat16
-    block = jax.ShapeDtypeStruct(q_fwd.shape, low)
     anywhere = pl.BlockSpec(memory_space=pl.ANY)
     sems = pltpu.SemaphoreType.DMA
     made = pl.pallas_call(
         kernel,
         name="relay",
-        out_shape=(jax.ShapeDtypeStruct(resid.shape, low),) + (block,) * 6,
-        in_specs=[anywhere] * 9,
-        out_specs=(anywhere,) * 7,
+        out_shape=(pltpu.VMEM(resid.shape, low),) + (pltpu.VMEM(q_fwd.shape, low),) * 6,
+        in_specs=[pl.BlockSpec(memory_space=pltpu.HBM)] * 9,
+        out_specs=(pl.BlockSpec(memory_space=pltpu.VMEM),) * 7,
         scratch_shapes=[
             pltpu.VMEM((features, width), low),
             pltpu.VMEM((slots, rows, width), low),
@@ -388,7 +370,6 @@
             pltpu.VMEM((rows, width - CUT), low),
             *[pltpu.VMEM((seq, features), low) for _ in range(6)],
             pltpu.VMEM((3, seq, features), low),
-            pltpu.VMEM((3, seq, features), low),
             pltpu.VMEM((rows, width), low),
             pltpu.VMEM((seq, features), low),
             pltpu.VMEM((seq, features), low),
@@ -396,9 +377,7 @@
             pltpu.VMEM((seq, features), low),
             pltpu.VMEM((seq, features), jnp.float32),
             pltpu.VMEM((seq, features), low),
-            pltpu.VMEM((3, seq, features), low),
-            pltpu.VMEM((rows, width), low),
-            sems((12,)), sems((7,)), sems((24,)), sems((24,)), sems((10,)), sems((10,)),
+            sems((12,)), sems((24,)), sems((24,)), sems((10,)), sems((10,)),
             sems((24,)), sems((24,)), sems((9,)), sems((9,)), sems((6,)), sems((6,)),
         ],
         compiler_params=pltpu.CompilerParams(
@@ -409,10 +388,10 @@
         place,
         name="place",
         out_shape=tuple(jax.ShapeDtypeStruct(x.shape, x.dtype) for x in made),
-        in_specs=[anywhere] * 7,
+        in_specs=[pl.BlockSpec(memory_space=pltpu.VMEM)] * 7,
         out_specs=(anywhere,) * 7,
-        scratch_shapes=[pltpu.VMEM(x.shape, x.dtype) for x in made] + [sems((7,)), sems((7,))],
-    )(*made)
+        scratch_shapes=[sems((7,))],
+    )(*(pltpu.with_memory_space_constraint(x, pltpu.VMEM) for x in made))
 
 
 def solution(mesh):

time: 114 us -> 109 us (0.956)
  Pallas kernels: 113 us -> 108 us
    pallas_call x1, Pallas kernels: 111 us -> 107 us  [per_device(): pl.pallas_call(kernel, name='relay', out_shape=(pltpu.VMEM(resid.shape, l...]
where the time goes in v3:
time: 109 us
  Pallas kernels  108 us (99%)
    pallas_call x1, Pallas kernels, per_device(): pl.pallas_call(kernel, name='relay', out_shape=(pltpu.VMEM(resid.shape, l...  107 us

profile of v3, /device:TPU:1, one launch (start us, length us, event | category | flops | bytes accessed | tf_op | source)
XLA Modules:
  0.0 108.8 jit_solution(14329730510958097954)
XLA Ops:
  0.6 107.0 %relay.1 = (bf16[1,16,12288]{2,1,0:T(8,128)(2,1)S(1)}, bf16[1,256,384]{2,1,0:T(8,128)(2,1)S(1)}, bf16[1,256,384]{2,1,0:T(8,128)(2,1)S(1)}, bf16[1,256,384]{2,1,0...) custom-call(bf16[1,256,384]{2,1,0:T(8,128)(2,1)} %q_in.1, ...), custom_call_target="tpu_custom_call" | custom-call | tf_op jit(solution)/shard_map/relay/pallas_call | solution.py:357
  107.6 1.2 %place.1 = (bf16[1,16,12288]{2,1,0:T(8,128)(2,1)}, bf16[1,256,384]{2,1,0:T(8,128)(2,1)}, bf16[1,256,384]{2,1,0:T(8,128)(2,1)}, bf16[1,256,384]{2,1,0:T(8,128)(2,...) custom-call(bf16[1,16,12288]{2,1,0:T(8,128)(2,1)S(1)} %get-tuple-element.14.refs_0_, ...), custom_call_target="tpu_custom_call" | custom-call | tf_op jit(solution)/shard_map/place/pallas_call | solution.py:387

commit v4 on v3

--- a/solution.py
+++ b/solution.py
@@ -54,6 +54,10 @@
         block = lax.rem(z + off % 8, 8) * 2 + lax.rem(line + side, 2)
         return pl.multiple_of(block * rows, rows)
 
+    barrier = pltpu.get_barrier_semaphore()
+    for device in (up, down, across, mirror):
+        pl.semaphore_signal(barrier, inc=1, device_id=device, device_id_type=MESH)
+
     loads = {}
 
     def load(name, src, dst):
@@ -61,14 +65,16 @@
         loads[name].start()
 
     load("cot", cot_in.at[0], g.at[slot(0, 0)])
-    for i, ref in enumerate((qp_in, kp_in, vp_in)):
-        load(f"p{i}", ref.at[0], parked.at[i])
     load("q", q_in.at[0], qf)
     load("k", k_in.at[0], kf)
     load("v", v_in.at[0], vf)
-    quarter = w.shape[0] // 4
-    for i in range(4):
-        load(f"w{i}", w_in.at[0, pl.ds(i * quarter, quarter)], w.at[pl.ds(i * quarter, quarter)])
+    deep = w.shape[0] // 2
+    for name, cols in (("b", pl.ds(CUT, wide_b)), ("a", pl.ds(0, CUT))):
+        for i in range(2):
+            depth = pl.ds(i * deep, deep)
+            load(f"w{name}{i}", w_in.at[0, depth, cols], w.at[depth, cols])
+    for i, ref in enumerate((qp_in, kp_in, vp_in)):
+        load(f"p{i}", ref.at[0], parked.at[i])
     load("resid", resid_in.at[0], resid)
 
     def remote(src, dst, send, recv, device):
@@ -256,14 +262,14 @@
             for name in ("q", "k", "v"):
                 loads[name].wait()
             forward_attention()
+            total[...] = jnp.zeros_like(total)
         elif what == "crossed":
             agy["b"].wait_recv()
             for way in range(2):
                 agz[way, 0, 2].start()
         elif what in ("project_b", "project_a"):
-            if what == next(step[0] for step in PLAN if step[0].startswith("project")):
-                for i in range(4):
-                    loads[f"w{i}"].wait()
+            for i in range(2):
+                loads[f"w{what[-1]}{i}"].wait()
             project(*((0, CUT) if what == "project_a" else (CUT, width)))
         elif what == "part":
             rsy[at[0]].start()
@@ -299,22 +305,10 @@
             spread_grad()
             backward_attention()
 
-    barrier = pltpu.get_barrier_semaphore()
-    for device in (up, down, across, mirror):
-        pl.semaphore_signal(barrier, inc=1, device_id=device, device_id_type=MESH)
     pl.semaphore_wait(barrier, 4)
-
     loads["cot"].wait()
-    total[...] = jnp.zeros_like(total)
     for step in PLAN:
         act(*step)
-
-    loads["resid"].wait()
-    rsy[0].wait_recv()
-    for way in range(2):
-        rsz[way, 3, 0].wait_recv()
-        rsz[way, 3, 1].wait_recv()
-    rsy["b"].wait_recv()
 
     def finish(first, last, refs, shift):
         @pl.loop(0, (last - first) // STEP)
@@ -325,16 +319,22 @@
                 total += ref[:, pl.ds(pl.multiple_of(first - shift + i * STEP, STEP), STEP)].astype(jnp.float32)
             out_ref[0, :, cols] = (resid[:, cols].astype(jnp.float32) + total).astype(jnp.bfloat16)
 
-    finish(0, CUT, (ya.at[0], za.at[0, 3], za.at[1, 3]), 0)
-    finish(CUT, width, (yb, zb.at[0, 3, 0], zb.at[1, 3, 0]), CUT)
-
-    for i in range(3, 6):
-        mir[i].wait_recv()
+    loads["resid"].wait()
     for copies in (agz, rsz, agy, rsy):
         for copy in copies.values():
             copy.wait_send()
     for copy in mir:
         copy.wait_send()
+    for i in range(3, 6):
+        mir[i].wait_recv()
+    rsy["b"].wait_recv()
+    for way in range(2):
+        rsz[way, 3, 1].wait_recv()
+    finish(CUT, width, (yb, zb.at[0, 3, 0], zb.at[1, 3, 0]), CUT)
+    rsy[0].wait_recv()
+    for way in range(2):
+        rsz[way, 3, 0].wait_recv()
+    finish(0, CUT, (ya.at[0], za.at[0, 3], za.at[1, 3]), 0)
 
 
 def place(*refs):

time: 109 us -> 108 us (level); the launches traced: 109 us -> 107 us
  Pallas kernels: 108 us -> 106 us
    pallas_call x1, Pallas kernels: 107 us -> 105 us  [per_device(): pl.pallas_call(kernel, name='relay', out_shape=(pltpu.VMEM(resid.shape, l...]
where the time goes in v4:
time: 108 us; the launch traced here: 107 us
  Pallas kernels  106 us (98%)
    pallas_call x1, Pallas kernels, per_device(): pl.pallas_call(kernel, name='relay', out_shape=(pltpu.VMEM(resid.shape, l...  105 us

profile of v4, /device:TPU:1, one launch (start us, length us, event | category | flops | bytes accessed | tf_op | source)
XLA Modules:
  0.0 106.6 jit_solution(1593357633743016042)
XLA Ops:
  0.6 104.8 %relay.1 = (bf16[1,16,12288]{2,1,0:T(8,128)(2,1)S(1)}, bf16[1,256,384]{2,1,0:T(8,128)(2,1)S(1)}, bf16[1,256,384]{2,1,0:T(8,128)(2,1)S(1)}, bf16[1,256,384]{2,1,0...) custom-call(bf16[1,256,384]{2,1,0:T(8,128)(2,1)} %q_in.1, ...), custom_call_target="tpu_custom_call" | custom-call | tf_op jit(solution)/shard_map/relay/pallas_call | solution.py:357
  105.4 1.2 %place.1 = (bf16[1,16,12288]{2,1,0:T(8,128)(2,1)}, bf16[1,256,384]{2,1,0:T(8,128)(2,1)}, bf16[1,256,384]{2,1,0:T(8,128)(2,1)}, bf16[1,256,384]{2,1,0:T(8,128)(2,...) custom-call(bf16[1,16,12288]{2,1,0:T(8,128)(2,1)S(1)} %get-tuple-element.14.refs_0_, ...), custom_call_target="tpu_custom_call" | custom-call | tf_op jit(solution)/shard_map/place/pallas_call | solution.py:387

commit v5 on v4

--- a/solution.py
+++ b/solution.py
@@ -155,11 +155,13 @@
                 ctxp[pl.ds(slot(off, side) * rows, rows), :] = ctx[pl.ds(row_of(off, side), rows), :]
 
     def project(first, last):
-        @pl.loop(first // TILE, last // TILE)
+        tile = 1792 if (last - first) % 1792 == 0 else 2560
+
+        @pl.loop(0, (last - first) // tile)
         def _(i):
-            cols = pl.ds(pl.multiple_of(i * TILE, TILE), TILE)
+            cols = pl.ds(pl.multiple_of(first + i * tile, HEAD), tile)
             made = jnp.dot(ctxp[...], w[:, cols], preferred_element_type=jnp.float32).astype(jnp.bfloat16)
-            part[:, :, cols] = made.reshape(part.shape[0], rows, TILE)
+            part[:, :, cols] = made.reshape(part.shape[0], rows, tile)
 
     def gather_grad(first, last):
         @pl.loop(first // TILE, last // TILE)

time: 108 us -> 108 us (level)
  no operation moved by 1% of the time
where the time goes in v5:
time: 108 us; the launch traced here: 107 us
  Pallas kernels  106 us (98%)
    pallas_call x1, Pallas kernels, per_device(): pl.pallas_call(kernel, name='relay', out_shape=(pltpu.VMEM(resid.shape, l...  105 us

profile of v5, /device:TPU:1, one launch (start us, length us, event | category | flops | bytes accessed | tf_op | source)
XLA Modules:
  0.0 106.6 jit_solution(11860628753317126983)
XLA Ops:
  0.6 104.8 %relay.1 = (bf16[1,16,12288]{2,1,0:T(8,128)(2,1)S(1)}, bf16[1,256,384]{2,1,0:T(8,128)(2,1)S(1)}, bf16[1,256,384]{2,1,0:T(8,128)(2,1)S(1)}, bf16[1,256,384]{2,1,0...) custom-call(bf16[1,256,384]{2,1,0:T(8,128)(2,1)} %q_in.1, ...), custom_call_target="tpu_custom_call" | custom-call | tf_op jit(solution)/shard_map/relay/pallas_call | solution.py:359
  105.4 1.2 %place.1 = (bf16[1,16,12288]{2,1,0:T(8,128)(2,1)}, bf16[1,256,384]{2,1,0:T(8,128)(2,1)}, bf16[1,256,384]{2,1,0:T(8,128)(2,1)}, bf16[1,256,384]{2,1,0:T(8,128)(2,...) custom-call(bf16[1,16,12288]{2,1,0:T(8,128)(2,1)S(1)} %get-tuple-element.14.refs_0_, ...), custom_call_target="tpu_custom_call" | custom-call | tf_op jit(solution)/shard_map/place/pallas_call | solution.py:389
